TPU v7x, 32 devices: a whole 2x2x4 slice. The times are simulated.
32 devices in a mesh: row: 4 (over y, x), col: 8 (over z, core).
Axes of the slice: x: 2, y: 2, z: 4, core: 2. Of those that a mesh axis runs over, the one named last changes fastest.
Arguments:
- amplitudes: bfloat16 [32, 256, 32, 256], P('row', None, 'col'), may hold values from -6 to 6
- factors: bfloat16 [32, 256, 384], P('row'), may hold values from -0.109375 to 0.109375
- occ_energy: float32 [32], replicated, may hold values from -2 to -0.5
- vir_energy: float32 [256], replicated, may hold values from 0.2 to 3
Outputs:
- residual: float32 [32, 256, 32, 256], P('row', None, 'col')
All inputs are finite; a program needn't handle non-finite values.
Results may differ from a plain program's by a relative error of at most 0.0029.
Values may be sent and summed in bfloat16 or wider, within the bound.
A program may use at most 192 MiB of HBM per device.

v0:
```python
import functools

import jax
import jax.numpy as jnp
from jax import lax
from jax.experimental import pallas as pl
from jax.experimental.pallas import tpu as pltpu
from jax.sharding import PartitionSpec as P

BF16 = jnp.bfloat16
F32 = jnp.float32


def denominators(occ_energy, vir_energy, rows, cols):
    row_place = lax.axis_index("row")
    col_place = lax.axis_index("col")
    occ_first = lax.dynamic_slice_in_dim(occ_energy, row_place * rows, rows, 0)
    occ_second = lax.dynamic_slice_in_dim(occ_energy, col_place * cols, cols, 0)
    return (
        vir_energy[None, :, None, None]
        + vir_energy[None, None, None, :]
        - occ_first[:, None, None, None]
        - occ_second[None, None, :, None]
    )


def coupling_of(left_one, right):
    count, virtual, _ = right.shape
    coulomb = lax.dot_general(
        left_one, right.reshape(count * virtual, -1), (((1,), (1,)), ((), ())), preferred_element_type=F32
    )
    exchange = lax.dot_general(right, left_one, (((2,), (1,)), ((), ())), preferred_element_type=F32)
    exchange = exchange.transpose(1, 0, 2).reshape(virtual, count * virtual)
    return (2.0 * coulomb - exchange).astype(BF16)


def general_body(amplitudes, factors, occ_energy, vir_energy):
    rows, virtual, cols, _ = amplitudes.shape
    all_factors = lax.all_gather(factors, "row", axis=0, tiled=True)
    all_amplitudes = lax.all_gather(amplitudes, "row", axis=0, tiled=True)
    columns = all_amplitudes.reshape(-1, cols * virtual)

    def one(left_one):
        return jnp.dot(coupling_of(left_one, all_factors), columns, preferred_element_type=F32)

    summed = lax.map(one, factors).reshape(rows, virtual, cols, virtual)
    swapped = summed.astype(BF16).transpose(2, 3, 0, 1)
    section_one = lax.all_to_all(swapped, "row", split_axis=1, concat_axis=2, tiled=True)
    section_two = lax.all_to_all(section_one, "col", split_axis=2, concat_axis=0, tiled=True)
    mirrored = lax.all_to_all(section_two, "row", split_axis=0, concat_axis=1, tiled=True)
    return (summed + mirrored) / denominators(occ_energy, vir_energy, rows, cols)


def coupling_block(left, right):
    wide_left = jnp.concatenate([left + left, -right], axis=1)
    wide_right = jnp.concatenate([right, left], axis=1)
    product = lax.dot_general(wide_left, wide_right, (((1,), (1,)), ((), ())), preferred_element_type=F32)
    return product.astype(BF16)


def flip(place, offset, ranks):
    result, bit = 0, 1
    while bit < ranks:
        one, two = (place // bit) % 2, (offset // bit) % 2
        result = result + bit * (one + two - 2 * one * two)
        bit *= 2
    return result


def exchange_kernel(
    ranks, factors_ref, parts_ref, direct_ref, mirror_ref,
    held, columns, coupling, total, sums, staged,
    local_sem, factor_send, factor_recv, part_send, part_recv, pass_send, pass_recv,
    direct_send, direct_recv, stage_send, stage_recv, mirror_send, mirror_recv,
):
    rows, virtual, _ = factors_ref.shape
    half = rows // 2
    depth = coupling.shape[1] // virtual
    row = lax.axis_index("row")
    col = lax.axis_index("col")
    plane, side = col // 2, col % 2
    twin = 2 * plane + 1 - side

    def remote(src, dst, send, recv, to_row, to_col):
        return pltpu.make_async_remote_copy(
            src_ref=src, dst_ref=dst, send_sem=send, recv_sem=recv,
            device_id=(to_row, to_col), device_id_type=pl.DeviceIdType.MESH,
        )

    barrier = pltpu.get_barrier_semaphore()
    peers = [(row, twin)]
    for d in range(1, ranks):
        peers += [(flip(row, d, ranks), col), (flip(row, d, ranks), twin), (row, 2 * flip(plane, d, ranks) + side)]
    for peer in peers:
        pl.semaphore_signal(barrier, inc=1, device_id=peer, device_id_type=pl.DeviceIdType.MESH)
    pl.semaphore_wait(barrier, len(peers))

    own_half = pl.ds(side * half, half)

    def factor_copy(d):
        return remote(factors_ref.at[own_half], held.at[d, own_half], factor_send.at[d], factor_recv.at[d], flip(row, d, ranks), col)

    def part_copy(d):
        return remote(parts_ref.at[flip(row, d, ranks)], columns.at[0, d], part_send.at[d], part_recv.at[d], flip(row, d, ranks), col)

    def pass_factor(d):
        return remote(held.at[d, own_half], held.at[d, own_half], pass_send.at[0, d], pass_recv.at[0, d], row, twin)

    def pass_part(d):
        src = parts_ref.at[row] if d == 0 else columns.at[0, d]
        return remote(src, columns.at[1, d], pass_send.at[1, d], pass_recv.at[1, d], row, twin)

    def factor_other(d):
        other_half = pl.ds((1 - side) * half, half)
        return remote(held.at[d, other_half], held.at[d, other_half], pass_send.at[0, d], pass_recv.at[0, d], row, twin)

    local = [
        pltpu.make_async_copy(factors_ref, held.at[0], local_sem.at[0]),
        pltpu.make_async_copy(parts_ref.at[row], columns.at[0, 0], local_sem.at[1]),
    ]
    for copy in local:
        copy.start()
    pass_part(0).start()
    near, far = list(range(1, ranks - 1)), ranks - 1
    for d in near:
        factor_copy(d).start()

    def direct_copy(d, h):
        to_col = col if h == 0 else twin
        return remote(sums.at[d, h], direct_ref.at[d, h], direct_send.at[d, h], direct_recv.at[d, h], flip(row, d, ranks), to_col)

    def stage_copy(d, h):
        goal = flip(row, d, ranks)
        slot = flip(plane, goal, ranks)
        copy = remote(
            sums.at[d, h], staged.at[slot, h], stage_send.at[slot, h], stage_recv.at[slot, h], row, 2 * goal + side
        )
        return slot, copy

    def keep_direct():
        return pltpu.make_async_copy(sums.at[0, 0], direct_ref.at[0, 0], local_sem.at[2])

    def keep_stage(d):
        return pltpu.make_async_copy(sums.at[d], staged.at[0], local_sem.at[3])

    def send_sums(d):
        for h in range(2):
            for u in range(half):
                sums[d, h, u] = total[h, d, u * virtual:(u + 1) * virtual, :].astype(BF16)
        for h in range(2):
            slot, copy = stage_copy(d, h)
            pl.when(slot != 0)(copy.start)
        pl.when(slot == 0)(lambda: keep_stage(d).start())
        for h in range(2):
            if d == 0 and h == 0:
                keep_direct().start()
            else:
                direct_copy(d, h).start()

    base = [(di, dk) for dk in range(far) for di in range(far)]
    crossing = [(d, far) for d in near]
    closing = [(far, dk) for dk in range(ranks)]
    middle_order = base + crossing + [(0, far)] + closing
    end_order = base + [(0, far)] + closing + crossing
    at_end = jnp.where((row == 0) | (row == far), 1, 0)

    def chosen(g, which):
        result = 0
        for spot, (one, two) in enumerate(zip(end_order, middle_order)):
            value = one[which] if one[which] == two[which] else at_end * one[which] + (1 - at_end) * two[which]
            result = result + jnp.where(g == spot, value, 0)
        return result

    def tile(g, carry):
        di, dk = chosen(g, 0), chosen(g, 1)

        @pl.when(g == 0)
        def _():
            for copy in local:
                copy.wait()
            pass_part(0).wait_recv()

        @pl.when(g == 1)
        def _():
            for d in near:
                factor_copy(d).wait_send()
                part_copy(d).start()
            for d in near:
                factor_copy(d).wait_recv()
                pass_factor(d).start()

        for d in near:
            @pl.when(g == d)
            def _():
                factor_other(d).wait_recv()

        @pl.when(g == far)
        def _():
            for d in near:
                part_copy(d).wait_send()
            factor_copy(far).start()
            part_copy(far).start()
            for d in near:
                part_copy(d).wait_recv()
                pass_part(d).start()

        for d in near:
            @pl.when(g == far * d)
            def _():
                pass_part(d).wait_recv()

        @pl.when(g == far * far - 1)
        def _():
            factor_copy(far).wait_recv()
            pass_factor(far).start()
            part_copy(far).wait_recv()
            pass_part(far).start()

        @pl.when(g == far * far)
        def _():
            factor_other(far).wait_recv()
            pass_part(far).wait_recv()

        pairs, steps = half // 2, rows // depth

        def inner(m, carry):
            place, step = 2 * (m // steps), m % steps
            for u in range(2):
                left = held[di, side * half + place + u]
                for e in range(depth):
                    block = coupling_block(left, held[dk, step * depth + e])
                    coupling[u * virtual:(u + 1) * virtual, e * virtual:(e + 1) * virtual] = block
            start = pl.multiple_of(step * depth * virtual, depth * virtual)
            spot = pl.ds(pl.multiple_of(place * virtual, 2 * virtual), 2 * virtual)
            fresh = jnp.where((dk == 0) & (step == 0), 1, 0)
            for h in range(2):
                part = jnp.dot(coupling[...], columns[h, dk, pl.ds(start, depth * virtual), :], preferred_element_type=F32)

                @pl.when(fresh == 1)
                def _():
                    total[h, di, spot, :] = part

                @pl.when(fresh == 0)
                def _():
                    total[h, di, spot, :] = total[h, di, spot, :] + part
            return carry

        lax.fori_loop(0, pairs * steps, inner, 0)

        for d in range(ranks):
            ends = [max(g for g, pair in enumerate(way) if pair[0] == d) for way in (end_order, middle_order)]

            @pl.when(g == at_end * ends[0] + (1 - at_end) * ends[1])
            def _():
                send_sums(d)
        return carry

    lax.fori_loop(0, ranks * ranks, tile, 0)

    def staged_copy(slot, h):
        return remote(sums.at[0, h], staged.at[slot, h], stage_send.at[slot, h], stage_recv.at[slot, h], row, twin)

    def mirror_copy(slot, place, h, goal):
        return remote(
            staged.at[slot, h], mirror_ref.at[place, h], mirror_send.at[place, h], mirror_recv.at[place, h], goal, col
        )

    def keep_mirror(slot, h):
        return pltpu.make_async_copy(staged.at[slot, h], mirror_ref.at[0, h], local_sem.at[4 + h])

    keep_stage(0).wait()
    for slot in range(ranks):
        goal = flip(plane, slot, ranks)
        place = flip(row, goal, ranks)
        for h in range(2):
            if slot > 0:
                staged_copy(slot, h).wait_recv()
            pl.when(place != 0)(mirror_copy(slot, place, h, goal).start)
            pl.when(place == 0)(keep_mirror(slot, h).start)

    keep_direct().wait()
    for h in range(2):
        keep_mirror(0, h).wait()
        for d in range(ranks):
            if d > 0 or h > 0:
                direct_copy(d, h).wait()
            if d > 0:
                staged_copy(d, h).wait_send()
                mirror_copy(0, d, h, row).wait()
    factor_copy(far).wait_send()
    part_copy(far).wait_send()
    for d in range(ranks):
        pass_part(d).wait_send()
        if d > 0:
            pass_factor(d).wait_send()


def exchanged_sums(factors, parts):
    rows, virtual, auxiliary = factors.shape
    ranks = parts.shape[0]
    half, depth = rows // 2, rows // 2
    shape = jax.ShapeDtypeStruct((ranks, 2, half, virtual, virtual), BF16)
    anywhere = pl.BlockSpec(memory_space=pl.ANY)
    dma = pltpu.SemaphoreType.DMA
    line, square = dma((ranks,)), dma((ranks, 2))
    across = dma((2, ranks))
    return pl.pallas_call(
        functools.partial(exchange_kernel, ranks),
        out_shape=(shape, shape),
        in_specs=[anywhere, anywhere],
        out_specs=(anywhere, anywhere),
        scratch_shapes=[
            pltpu.VMEM((ranks, rows, virtual, auxiliary), BF16),
            pltpu.VMEM((2, ranks, rows * virtual, virtual), BF16),
            pltpu.VMEM((2 * virtual, depth * virtual), BF16),
            pltpu.VMEM((2, ranks, half * virtual, virtual), F32),
            pltpu.VMEM((ranks, 2, half, virtual, virtual), BF16),
            pltpu.VMEM((ranks, 2, half, virtual, virtual), BF16),
            dma((6,)), line, line, line, line, across, across, square, square, square, square, square, square,
        ],
        compiler_params=pltpu.CompilerParams(
            collective_id=0, has_side_effects=True, vmem_limit_bytes=56 * 1024 * 1024
        ),
    )(factors, parts)


def combine_kernel(ranks, place_ref, occ_ref, direct_ref, mirror_ref, vir_col_ref, vir_row_ref, out_ref):
    step = pl.program_id(0)
    row, col = place_ref[0], place_ref[1]
    cols = out_ref.shape[2]
    rows = pl.num_programs(0)
    pair_sum = vir_col_ref[...] + vir_row_ref[...]
    first = occ_ref[row * rows + step]
    for j in range(cols):
        mine = direct_ref[flip(row, j, ranks), 0, 0].astype(F32)
        turned = mirror_ref[0, 0, j].astype(F32).T
        out_ref[0, :, j, :] = (mine + turned) / (pair_sum - first - occ_ref[col * cols + j])


def combined(direct, mirror, occ_energy, vir_energy):
    ranks, _, half, virtual, _ = direct.shape
    rows = 2 * half

    def spot(step, place_ref):
        h = lax.rem(step // half + place_ref[1], 2)
        return h, lax.rem(step, half)

    def direct_map(step, place_ref, occ_ref):
        h, u = spot(step, place_ref)
        return 0, h, u, 0, 0

    def mirror_map(step, place_ref, occ_ref):
        h, q = spot(step, place_ref)
        return flip(place_ref[0], q, ranks), h, 0, 0, 0

    place = jnp.stack([lax.axis_index("row"), lax.axis_index("col")]).astype(jnp.int32)
    grid_spec = pltpu.PrefetchScalarGridSpec(
        num_scalar_prefetch=2,
        grid=(rows,),
        in_specs=[
            pl.BlockSpec((ranks, 1, 1, virtual, virtual), direct_map),
            pl.BlockSpec((1, 1, half, virtual, virtual), mirror_map),
            pl.BlockSpec((virtual, 1), lambda step, *_: (0, 0)),
            pl.BlockSpec((1, virtual), lambda step, *_: (0, 0)),
        ],
        out_specs=pl.BlockSpec((1, virtual, half, virtual), lambda step, *_: (step, 0, 0, 0)),
    )
    return pl.pallas_call(
        functools.partial(combine_kernel, ranks),
        out_shape=jax.ShapeDtypeStruct((rows, virtual, half, virtual), F32),
        grid_spec=grid_spec,
        compiler_params=pltpu.CompilerParams(vmem_limit_bytes=58 * 1024 * 1024),
    )(place, occ_energy, direct, mirror, vir_energy[:, None], vir_energy[None, :])


def paired_body(amplitudes, factors, occ_energy, vir_energy):
    rows, virtual, cols, _ = amplitudes.shape
    parts = amplitudes.transpose(2, 0, 1, 3).reshape(cols, rows * virtual, virtual)
    direct, mirror = exchanged_sums(factors, parts)
    return combined(direct, mirror, occ_energy, vir_energy)


def solution(mesh):
    ranks, places = mesh.shape["row"], mesh.shape["col"]

    def body(amplitudes, factors, occ_energy, vir_energy):
        rows, _, cols, _ = amplitudes.shape
        paired = places == 2 * ranks and rows == 2 * cols and cols == ranks and ranks in (4, 8)
        chosen = paired_body if paired else general_body
        return chosen(amplitudes, factors, occ_energy, vir_energy)

    in_specs = (P("row", None, "col", None), P("row", None, None), P(), P())
    out_specs = P("row", None, "col", None)
    return jax.shard_map(body, mesh=mesh, in_specs=in_specs, out_specs=out_specs, check_vma=False)
```

profile of v0, /device:TPU:18, one launch (start us, length us, event | category | flops | bytes accessed | tf_op | source)
XLA Modules:
  0.0 279.8 jit_solution(10754341835014899003)
XLA Ops:
  0.0 0.6 pad_add_fusion.place_ref
  0.6 1.5 copy.7.vir_col_ref
  2.1 5.0 %copy.6 = bf16[4,8,256,256]{3,2,1,0:T(8,128)(2,1)} copy(bf16[4,8,256,256]{3,0,2,1:T(4,128)(2,1)} %bitcast.7) | data formatting | bytes 8388608 | tf_op jit(solution)/shard_map/transpose | solution.py:378
  7.1 261.6 %shard_map.46 = (bf16[4,2,4,256,256]{4,3,2,1,0:T(8,128)(2,1)}, bf16[4,2,4,256,256]{4,3,2,1,0:T(8,128)(2,1)}) custom-call(bf16[8,256,384]{2,1,0:T(8,128)(2,1)} %factors_ref.1, bf16[4,2048,256]{2,1,0:T(8,128)(2,1)} %bitcast.6), custom_call_target="tpu_custom_call" | custom-call | tf_op jit(solution)/shard_map/pallas_call | solution.py:307
  268.7 11.1 %shard_map.47 = f32[8,256,4,256]{3,2,1,0:T(4,128)} custom-call(s32[2]{0:T(128)} %pad_add_fusion.place_ref, f32[32]{0:T(128)} %occ_ref.1, bf16[4,2,4,256,256]{4,3,2,1,0:T(8,128)(2,1)} %get-tuple-element.7.direct_ref, bf16[4,2,4,256,256]{4,3,2,1,0:T(8,128)(2,1)} %get-tuple-element.8.mirror_ref, f32[256,1]{1,0:T(8,128)} %copy.7.vir_col_ref, f32[1,256]{1,0:T(1,128)} %bitcast.9), custom_call_target="tpu_custom_call" | custom-call | tf_op jit(solution)/shard_map/pallas_call | solution.py:368
where the time goes:
time: 282 us; the launch traced here: 280 us
  Pallas kernels  273 us (97%)
  local copies, waits for them, and re-layouts  6.44 us (2%)
    pallas_call x1, Pallas kernels, exchanged_sums(): pl.pallas_call(functools.partial(exchange_kernel, ranks), out_shape=(shap...  262 us
    pallas_call x1, Pallas kernels, combined(): pl.pallas_call(functools.partial(combine_kernel, ranks), out_shape=jax.Sh...  11.1 us

commit v1 on v0

--- a/solution.py
+++ b/solution.py
@@ -122,8 +122,10 @@
         copy.start()
     pass_part(0).start()
     near, far = list(range(1, ranks - 1)), ranks - 1
-    for d in near:
+    turned = [side * (ranks - 1 - d) + (1 - side) * d for d in near]
+    for d in turned:
         factor_copy(d).start()
+    total[...] = jnp.zeros_like(total)
 
     def direct_copy(d, h):
         to_col = col if h == 0 else twin
@@ -161,7 +163,7 @@
     crossing = [(d, far) for d in near]
     closing = [(far, dk) for dk in range(ranks)]
     middle_order = base + crossing + [(0, far)] + closing
-    end_order = base + [(0, far)] + closing + crossing
+    end_order = base + [(0, far)] + crossing[::-1] + closing
     at_end = jnp.where((row == 0) | (row == far), 1, 0)
 
     def chosen(g, which):
@@ -182,7 +184,7 @@
 
         @pl.when(g == 1)
         def _():
-            for d in near:
+            for d in turned:
                 factor_copy(d).wait_send()
                 part_copy(d).start()
             for d in near:
@@ -232,17 +234,9 @@
                     coupling[u * virtual:(u + 1) * virtual, e * virtual:(e + 1) * virtual] = block
             start = pl.multiple_of(step * depth * virtual, depth * virtual)
             spot = pl.ds(pl.multiple_of(place * virtual, 2 * virtual), 2 * virtual)
-            fresh = jnp.where((dk == 0) & (step == 0), 1, 0)
             for h in range(2):
                 part = jnp.dot(coupling[...], columns[h, dk, pl.ds(start, depth * virtual), :], preferred_element_type=F32)
-
-                @pl.when(fresh == 1)
-                def _():
-                    total[h, di, spot, :] = part
-
-                @pl.when(fresh == 0)
-                def _():
-                    total[h, di, spot, :] = total[h, di, spot, :] + part
+                total[h, di, spot, :] += part
             return carry
 
         lax.fori_loop(0, pairs * steps, inner, 0)

time: 282 us -> 245 us (0.87)
  Pallas kernels: 273 us -> 233 us
    pallas_call x1, Pallas kernels: 262 us -> 222 us  [exchanged_sums(): pl.pallas_call(functools.partial(exchange_kernel, ranks), out_shape=(shap...]
where the time goes in v1:
time: 245 us; the launch traced here: 240 us
  Pallas kernels  233 us (95%)
  local copies, waits for them, and re-layouts  6.44 us (3%)
    pallas_call x1, Pallas kernels, exchanged_sums(): pl.pallas_call(functools.partial(exchange_kernel, ranks), out_shape=(shap...  222 us
    pallas_call x1, Pallas kernels, combined(): pl.pallas_call(functools.partial(combine_kernel, ranks), out_shape=jax.Sh...  11.1 us
    transpose x1, local copies, waits for them, and re-layouts, paired_body(): amplitudes.transpose(2, 0, 1, 3).reshape(cols, rows * virtual, virtual)  4.96 us

profile of v1, /device:TPU:18, one launch (start us, length us, event | category | flops | bytes accessed | tf_op | source)
XLA Modules:
  0.0 240.5 jit_solution(17663119801902487365)
XLA Ops:
  0.0 0.6 pad_add_fusion.place_ref
  0.6 1.5 copy.7.vir_col_ref
  2.1 5.0 %copy.6 = bf16[4,8,256,256]{3,2,1,0:T(8,128)(2,1)} copy(bf16[4,8,256,256]{3,0,2,1:T(4,128)(2,1)} %bitcast.7) | data formatting | bytes 8388608 | tf_op jit(solution)/shard_map/transpose | solution.py:372
  7.1 222.3 %shard_map.46 = (bf16[4,2,4,256,256]{4,3,2,1,0:T(8,128)(2,1)}, bf16[4,2,4,256,256]{4,3,2,1,0:T(8,128)(2,1)}) custom-call(bf16[8,256,384]{2,1,0:T(8,128)(2,1)} %factors_ref.1, bf16[4,2048,256]{2,1,0:T(8,128)(2,1)} %bitcast.6), custom_call_target="tpu_custom_call" | custom-call | tf_op jit(solution)/shard_map/pallas_call | solution.py:301
  229.3 11.1 %shard_map.47 = f32[8,256,4,256]{3,2,1,0:T(4,128)} custom-call(s32[2]{0:T(128)} %pad_add_fusion.place_ref, f32[32]{0:T(128)} %occ_ref.1, bf16[4,2,4,256,256]{4,3,2,1,0:T(8,128)(2,1)} %get-tuple-element.7.direct_ref, bf16[4,2,4,256,256]{4,3,2,1,0:T(8,128)(2,1)} %get-tuple-element.8.mirror_ref, f32[256,1]{1,0:T(8,128)} %copy.7.vir_col_ref, f32[1,256]{1,0:T(1,128)} %bitcast.9), custom_call_target="tpu_custom_call" | custom-call | tf_op jit(solution)/shard_map/pallas_call | solution.py:362

commit v2 on v1

--- a/solution.py
+++ b/solution.py
@@ -163,7 +163,7 @@
     crossing = [(d, far) for d in near]
     closing = [(far, dk) for dk in range(ranks)]
     middle_order = base + crossing + [(0, far)] + closing
-    end_order = base + [(0, far)] + crossing[::-1] + closing
+    end_order = base + [(0, far), crossing[-1]] + closing + crossing[:-1]
     at_end = jnp.where((row == 0) | (row == far), 1, 0)
 
     def chosen(g, which):
@@ -223,23 +223,19 @@
             factor_other(far).wait_recv()
             pass_part(far).wait_recv()
 
-        pairs, steps = half // 2, rows // depth
-
-        def inner(m, carry):
-            place, step = 2 * (m // steps), m % steps
-            for u in range(2):
-                left = held[di, side * half + place + u]
+        def inner(step, carry):
+            for u in range(half):
+                left = held[di, side * half + u]
                 for e in range(depth):
                     block = coupling_block(left, held[dk, step * depth + e])
                     coupling[u * virtual:(u + 1) * virtual, e * virtual:(e + 1) * virtual] = block
             start = pl.multiple_of(step * depth * virtual, depth * virtual)
-            spot = pl.ds(pl.multiple_of(place * virtual, 2 * virtual), 2 * virtual)
             for h in range(2):
                 part = jnp.dot(coupling[...], columns[h, dk, pl.ds(start, depth * virtual), :], preferred_element_type=F32)
-                total[h, di, spot, :] += part
+                total[h, di] += part
             return carry
 
-        lax.fori_loop(0, pairs * steps, inner, 0)
+        lax.fori_loop(0, rows // depth, inner, 0)
 
         for d in range(ranks):
             ends = [max(g for g, pair in enumerate(way) if pair[0] == d) for way in (end_order, middle_order)]
@@ -306,7 +302,7 @@
         scratch_shapes=[
             pltpu.VMEM((ranks, rows, virtual, auxiliary), BF16),
             pltpu.VMEM((2, ranks, rows * virtual, virtual), BF16),
-            pltpu.VMEM((2 * virtual, depth * virtual), BF16),
+            pltpu.VMEM((half * virtual, depth * virtual), BF16),
             pltpu.VMEM((2, ranks, half * virtual, virtual), F32),
             pltpu.VMEM((ranks, 2, half, virtual, virtual), BF16),
             pltpu.VMEM((ranks, 2, half, virtual, virtual), BF16),
@@ -327,7 +323,7 @@
     first = occ_ref[row * rows + step]
     for j in range(cols):
         mine = direct_ref[flip(row, j, ranks), 0, 0].astype(F32)
-        turned = mirror_ref[0, 0, j].astype(F32).T
+        turned = mirror_ref[0, 0, j].T.astype(F32)
         out_ref[0, :, j, :] = (mine + turned) / (pair_sum - first - occ_ref[col * cols + j])
 
 

time: 245 us -> 240 us (0.980); the launches traced: 240 us -> 239 us
  no operation moved by 1% of the time
where the time goes in v2:
time: 240 us; the launch traced here: 239 us
  Pallas kernels  232 us (97%)
  local copies, waits for them, and re-layouts  6.44 us (3%)
    pallas_call x1, Pallas kernels, exchanged_sums(): pl.pallas_call(functools.partial(exchange_kernel, ranks), out_shape=(shap...  221 us
    pallas_call x1, Pallas kernels, combined(): pl.pallas_call(functools.partial(combine_kernel, ranks), out_shape=jax.Sh...  11 us
    transpose x1, local copies, waits for them, and re-layouts, paired_body(): amplitudes.transpose(2, 0, 1, 3).reshape(cols, rows * virtual, virtual)  4.96 us

profile of v2, /device:TPU:18, one launch (start us, length us, event | category | flops | bytes accessed | tf_op | source)
XLA Modules:
  0.0 239.2 jit_solution(5662692801809697667)
XLA Ops:
  0.0 0.6 pad_add_fusion.place_ref
  0.6 1.5 copy.7.vir_col_ref
  2.1 5.0 %copy.6 = bf16[4,8,256,256]{3,2,1,0:T(8,128)(2,1)} copy(bf16[4,8,256,256]{3,0,2,1:T(4,128)(2,1)} %bitcast.7) | data formatting | bytes 8388608 | tf_op jit(solution)/shard_map/transpose | solution.py:368
  7.1 221.1 %shard_map.46 = (bf16[4,2,4,256,256]{4,3,2,1,0:T(8,128)(2,1)}, bf16[4,2,4,256,256]{4,3,2,1,0:T(8,128)(2,1)}) custom-call(bf16[8,256,384]{2,1,0:T(8,128)(2,1)} %factors_ref.1, bf16[4,2048,256]{2,1,0:T(8,128)(2,1)} %bitcast.6), custom_call_target="tpu_custom_call" | custom-call | tf_op jit(solution)/shard_map/pallas_call | solution.py:297
  228.2 11.0 %shard_map.47 = f32[8,256,4,256]{3,2,1,0:T(4,128)} custom-call(s32[2]{0:T(128)} %pad_add_fusion.place_ref, f32[32]{0:T(128)} %occ_ref.1, bf16[4,2,4,256,256]{4,3,2,1,0:T(8,128)(2,1)} %get-tuple-element.7.direct_ref, bf16[4,2,4,256,256]{4,3,2,1,0:T(8,128)(2,1)} %get-tuple-element.8.mirror_ref, f32[256,1]{1,0:T(8,128)} %copy.7.vir_col_ref, f32[1,256]{1,0:T(1,128)} %bitcast.9), custom_call_target="tpu_custom_call" | custom-call | tf_op jit(solution)/shard_map/pallas_call | solution.py:358
